TPU v7x, 512 devices: a whole 4x8x8 slice. The times are simulated.
512 devices in a mesh: dp: 4 (over x), expert: 128 (over z, y, core).
Axes of the slice: x: 4, y: 8, z: 8, core: 2. Of those that a mesh axis runs over, the one named last changes fastest.
Arguments:
- residual: bfloat16 [32768, 1024], P(('dp', 'expert')), parts along dimension 0, may hold values from -6 to 6
- expert_ids: int32 [32768, 8], P(('dp', 'expert')), parts along dimension 0, may hold values from 0 to 63, all different within a row; in each aligned block of 64 rows (0 to 63, 64 to 127, ...) at most 12 rows name the same one
- route_weights: float32 [32768, 8], P(('dp', 'expert')), parts along dimension 0, may hold values from 0.05 to 0.5
- expert_out: bfloat16 [393216, 1024], P(('dp', 'expert')), parts along dimension 0, may hold values from -6 to 6
Outputs:
- mixed: bfloat16 [32768, 1024], P(('dp', 'expert')), parts along dimension 0
- expert_load: float32 [256], P('dp'), parts along dimension 0
There are 4 independent parts, one for each index of `dp`. A program takes and returns all parts, laid end to end along the dimension named above; each array names one. Nothing has to cross between parts.
Inputs may be any that keep to these rules, and one draw needn't show every extreme that they name: `expert_ids`: each row names 8 different experts. Within the rows of one device no expert is named by more than 12 rows, and in some devices' rows an expert is named by exactly 12.
All inputs are finite; a program needn't handle non-finite values.
Results may differ from a plain program's by a relative error of at most 0.001.
Values may be sent and summed in bfloat16 or wider, within the bound.
No kernel may reach another device: no remote copies, remote signals or barrier semaphores. Data moves between devices by JAX's collectives and lax.ppermute only.
A program may use at most 64 MiB of HBM per device.

v0:
```python
import jax
import jax.numpy as jnp
from jax import lax
from jax.sharding import PartitionSpec as P

EXPERTS = 64


def per_device(residual, expert_ids, route_weights, expert_out):
    peers = lax.axis_size("expert")
    per_peer = expert_out.shape[0] // peers
    width = residual.shape[1]
    tokens_here = expert_ids.shape[0]
    fanout = expert_ids.shape[1]
    capacity = expert_out.shape[0] // EXPERTS
    routes = expert_ids.reshape(-1)
    onehot = (routes[:, None] == jnp.arange(EXPERTS, dtype=jnp.int32)[None, :]).astype(jnp.int32)
    earlier = jnp.cumsum(onehot, axis=0, dtype=jnp.int32) - onehot
    slots = jnp.sum(earlier * onehot, axis=1, dtype=jnp.int32)
    source_rows = routes * capacity + slots
    own_counts = jnp.sum(onehot, axis=0).astype(jnp.float32)
    column_blocks = 2
    block_width = width // column_blocks
    blocks = expert_out.reshape(peers, per_peer, column_blocks, block_width)
    count_row = jnp.zeros((width,), jnp.float32).at[:EXPERTS].set(own_counts)
    count_row = count_row.astype(jnp.bfloat16).reshape(1, 1, column_blocks, block_width)
    blocks = jnp.concatenate(
        [blocks, jnp.broadcast_to(count_row, (peers, 1, column_blocks, block_width))], axis=1
    )
    arrived = lax.all_to_all(blocks, "expert", split_axis=0, concat_axis=0, tiled=True)
    several = arrived.shape[2]
    payload = arrived[:, :per_peer]
    stacked = payload.reshape(peers * per_peer, several, arrived.shape[3])
    picked = jnp.take(stacked, source_rows, axis=0).reshape(
        tokens_here, fanout, several, arrived.shape[3]
    )
    total = jnp.zeros((tokens_here, several, arrived.shape[3]), jnp.float32)
    for choice_index in range(fanout):
        total = total + route_weights[:, choice_index, None, None] * picked[:, choice_index].astype(
            jnp.float32
        )
    count_sum = jnp.sum(arrived[:, per_peer].astype(jnp.float32), axis=0)
    result = (total, count_sum[None])
    summed, count_sum = result
    load_totals = count_sum.reshape(-1)[:EXPERTS]
    mixed = (summed.reshape(tokens_here, width) + residual.astype(jnp.float32)).astype(jnp.bfloat16)
    return (mixed, load_totals)


def solution(mesh):
    placed = (
        P(("dp", "expert"), None),
        P(("dp", "expert"), None),
        P(("dp", "expert"), None),
        P(("dp", "expert"), None),
    )
    return jax.shard_map(
        per_device,
        mesh=mesh,
        in_specs=placed,
        out_specs=(P(("dp", "expert"), None), P("dp")),
        check_vma=False,
    )
```

profile of v0, /device:TPU:6, one launch (start us, length us, event | category | flops | bytes accessed | tf_op | source)
XLA Modules:
  0.0 84.9 jit_solution(13101783865616272987)
XLA Ops:
  0.6 0.8 copy.23
  1.4 0.1 eq.26
  1.5 0.1 reshape.129
  1.6 1.2 %reduce-window.6 = s32[64,4,128]{2,0,1:T(8,128)S(1)} reduce-window(s32[64,4,128]{2,0,1:T(8,128)S(1)} %fusion.2, s32[]{:T(128)} %constant.45.clone.1), window={size=1x1x128 pad=0_0x0_0x127_0}, to_apply=%region_0.0 | reduce-window | flops 4161536 | bytes 262148 | tf_op jit(solution)/shard_map/reduce-window
  2.8 0.2 slice_reduce_fusion
  3.1 0.2 fusion.1
  3.3 2.9 %reshape.131 = bf16[128,6,2,512]{3,2,1,0:T(2,128)(2,1)S(1)} reshape(bf16[768,1024]{1,0:T(8,128)(2,1)} %param.9) | data formatting | bytes 3145728 | tf_op jit(solution)/shard_map/reshape | solution.py:24
  6.2 0.1 broadcast_in_dim.21
  6.3 3.6 %pad_maximum_fusion = bf16[128,7,2,512]{3,2,1,0:T(2,128)(2,1)} fusion(bf16[128,1,2,512]{3,2,1,0:T(2,128)(2,1)S(1)} %broadcast_in_dim.21, bf16[128,6,2,512]{3,2,1,0:T(2,128)(2,1)S(1)} %reshape.131), kind=kLoop, calls=%fused_computation.1 | loop fusion | flops 917504 | bytes 3670016 | tf_op jit(solution)/shard_map/concatenate | solution.py:27
  9.9 0.0 copy-start.1
  9.9 0.0 copy-start.2
  9.9 18.1 %all-to-all-start = ((bf16[128,7,2,512]{3,2,1,0:T(2,128)(2,1)}), bf16[128,7,2,512]{3,2,1,0:T(2,128)(2,1)S(1)}, u32[]{:S(2)}, u32[]{:S(2)}) async-start(bf16[128,7,2,512]{3,2,1,0:T(2,128)(2,1)} %pad_maximum_fusion), calls=%async_computation | async-start | bytes 3670016 | tf_op jit(solution)/shard_map/all_to_all | solution.py:30
  28.1 0.0 copy-done.1
  28.1 0.1 copy.27
  28.2 0.1 mul.115
  28.3 0.1 reduce_sum.32
  28.4 0.1 copy.26
  28.5 0.0 copy-done.2
  28.5 46.4 %all-to-all-done = bf16[128,7,2,512]{3,2,1,0:T(2,128)(2,1)S(1)} async-done(((bf16[128,7,2,512]{3,2,1,0:T(2,128)(2,1)}), bf16[128,7,2,512]{3,2,1,0:T(2,128)(2,1)S(1)}, u32[]{:S(2)}, u32[]{:S(2)}) %all-to-all-start) | async-done | bytes 1835040 | tf_op jit(solution)/shard_map/all_to_all | solution.py:30
  74.9 0.3 convert_reduce_fusion
  75.2 0.5 slice.94
  75.7 1.1 %slice.98 = bf16[128,6,2,512]{3,2,1,0:T(2,128)(2,1)S(1)} slice(bf16[128,7,2,512]{3,2,1,0:T(2,128)(2,1)S(1)} %all-to-all-done), slice={[0:128], [0:6], [0:2], [0:512]} | slice | bytes 3145728 | tf_op jit(solution)/shard_map/slice | solution.py:32
  76.8 3.6 %gather_fusion = bf16[512,2,512]{2,1,0:T(2,128)(2,1)S(1)} fusion(bf16[768,2,512]{2,1,0:T(2,128)(2,1)S(1)} %bitcast.65, s32[1024]{0:T(1024)S(1)} %pad_clamp_fusion), kind=kCustom, calls=%fused_computation | custom fusion | bytes 2099200 | tf_op jit(solution)/shard_map/jit(_take)/gather | solution.py:34
  80.3 1.2 %copy_select_fusion = bf16[64,8,2,512]{3,0,2,1:T(8,128)(2,1)S(1)} fusion(bf16[64,8,2,512]{3,2,1,0:T(2,128)(2,1)S(1)} %bitcast.66, pred[64,8]{0,1:T(8,128)(4,1)S(1)} %compare_and_fusion), kind=kLoop, calls=%fused_computation.2 | loop fusion | flops 524288 | bytes 2097664 | tf_op jit(solution)/shard_map/jit(_take)/select_n | solution.py:34
  81.6 0.2 slice_convert_fusion.7
  81.8 0.2 copy.30
  82.1 0.2 copy.37
  82.3 0.2 copy.36
  82.6 0.2 copy.35
  82.9 0.2 copy.34
  83.1 0.0 copy-start
  83.2 0.2 copy.33
  83.4 0.2 copy.32
  83.7 0.2 copy.31
  84.0 0.0 copy-done
  84.0 0.9 %add_convert_fusion = bf16[64,1024]{1,0:T(8,128)(2,1)} fusion(bf16[64,1024]{1,0:T(8,128)(2,1)S(1)} %copy-done, f32[64,1024]{1,0:T(8,128)S(1)} %bitcast.68, f32[64,1024]{1,0:T(8,128)S(1)} %bitcast.69, f32[64,1024]{1,0:T(8,128)S(1)} %bitcast.70, f32[64,1024]{1,0:T(8,128)S(1)} %bitcast.71, f32[64,1024]{1,0:T(8,128)S(1)} %bitcast.72, f32[64,1024]{1,0:T(8,128)S(1)} %bitcast.73, ...), kind=kLoop, calls=%fused_computation.4 | loop fusion | flops 1179648 | bytes 2361344 | tf_op jit(solution)/shard_map/convert_element_type | solution.py:46
  (20 shorter events, 0.5 us)
Async XLA Ops:
  9.9 18.1 %copy-start.1 = (s32[64,8]{0,1:T(8,128)S(1)}, s32[64,8]{0,1:T(8,128)}, u32[]{:S(2)}) copy-start(s32[64,8]{0,1:T(8,128)} %param.7) | copy-start | bytes 6148
  9.9 18.5 %copy-start.2 = (f32[64,8]{0,1:T(8,128)S(1)}, f32[64,8]{0,1:T(8,128)}, u32[]{:S(2)}) copy-start(f32[64,8]{0,1:T(8,128)} %param.8) | copy-start | bytes 6148
  9.9 65.0 %all-to-all-start = ((bf16[128,7,2,512]{3,2,1,0:T(2,128)(2,1)}), bf16[128,7,2,512]{3,2,1,0:T(2,128)(2,1)S(1)}, u32[]{:S(2)}, u32[]{:S(2)}) async-start(bf16[128,7,2,512]{3,2,1,0:T(2,128)(2,1)} %pad_maximum_fusion), calls=%async_computation | async-start | bytes 3670016 | tf_op jit(solution)/shard_map/all_to_all | solution.py:30
  83.1 0.9 %copy-start = (bf16[64,1024]{1,0:T(8,128)(2,1)S(1)}, bf16[64,1024]{1,0:T(8,128)(2,1)}, u32[]{:S(2)}) copy-start(bf16[64,1024]{1,0:T(8,128)(2,1)} %param.6) | copy-start | bytes 393220
where the time goes:
time: 86 us; the launch traced here: 84.9 us
  waiting for transfers between devices  46.4 us (54%)
  starting transfers between devices  18.1 us (21%)
  local copies, waits for them, and re-layouts  11.8 us (14%)
  other arithmetic  7.69 us (9%)
  between operations  0.88 us (1%)
    all_to_all x1, waiting for transfers between devices, per_device(): lax.all_to_all(blocks, 'expert', split_axis=0, concat_axis=0, tiled=True)  46.4 us
    all_to_all x1, starting transfers between devices, per_device(): lax.all_to_all(blocks, 'expert', split_axis=0, concat_axis=0, tiled=True)  18.1 us
    concatenate x1, other arithmetic, per_device(): jnp.concatenate([blocks, jnp.broadcast_to(count_row, (peers, 1, column_bl...  3.63 us
    gather x1, local copies, waits for them, and re-layouts, per_device(): jnp.take(stacked, source_rows, axis=0)  3.56 us
    reshape x1, local copies, waits for them, and re-layouts, per_device(): blocks = expert_out.reshape(peers, per_peer, column_blocks, block_width)  2.88 us
  transfers between devices with their start and end apart: 1, of which 1 were waited for; matrix products, arithmetic and copies ran while one was open for 0% of the time, Pallas kernels for 0%

commit v1 on v0

v1 whole, which is shorter than its diff:
```python
import jax
import jax.numpy as jnp
from jax import lax
from jax.experimental import pallas as pl
from jax.experimental.pallas import tpu as pltpu
from jax.sharding import PartitionSpec as P

EXPERTS = 64
TOP = 8
TOK = 64
HELD = 6
PEERS = 128
COLS = 256
UNITS = 3
GROUP = 16
VMEM = 24 * 2**20


def iota(shape, dim):
    return lax.broadcasted_iota(jnp.int32, shape, dim)


def pack_kernel(x_hbm, ids_hbm, out_ref, counts_ref, x_ref, ids_ref, x_sems, ids_sem):
    rows = GROUP * HELD
    groups = PEERS // GROUP
    x_copies = [
        pltpu.make_async_copy(
            x_hbm.at[pl.ds(g * rows, rows)], x_ref.at[pl.ds(g * rows, rows)], x_sems.at[g]
        )
        for g in range(groups)
    ]
    ids_copy = pltpu.make_async_copy(ids_hbm, ids_ref, ids_sem)
    ids_copy.start()
    for copy in x_copies:
        copy.start()
    line, column = iota((GROUP * 8, 2 * rows), 0), iota((GROUP * 8, 2 * rows), 1)
    owner, r = GROUP - 1 - line // 8, line % 8
    pick = []
    for u in range(UNITS):
        wanted = jnp.where(r < HELD, HELD * owner + r, rows + HELD * owner + 2 * u + r - HELD)
        pick.append((column == wanted).astype(jnp.float32).astype(jnp.bfloat16))
    ids_copy.wait()
    expert = iota((EXPERTS, TOK), 0)
    named = jnp.zeros((EXPERTS, TOK), jnp.float32)
    for k in range(TOP):
        named = named + (ids_ref[k : k + 1, :] == expert).astype(jnp.float32)
    counts_ref[...] = lax.dot_general(
        jnp.ones((8, TOK), jnp.bfloat16),
        named.astype(jnp.bfloat16),
        (((1,), (1,)), ((), ())),
        preferred_element_type=jnp.float32,
    )
    for g in range(groups):
        x_copies[g].wait()
        here = pl.ds(g * rows, rows)
        last = x_ref[here, UNITS * COLS :]
        for u in range(UNITS):
            source = jnp.concatenate([x_ref[here, u * COLS : (u + 1) * COLS], last], axis=0)
            packed = jnp.dot(pick[u], source, preferred_element_type=jnp.float32)
            out_ref[pl.ds((groups - 1 - g) * GROUP, GROUP), u] = packed.astype(
                jnp.bfloat16
            ).reshape(GROUP, 8, COLS)


def weights_kernel(ids_ref, route_ref, out_ref):
    expert = iota((EXPERTS, TOK), 0)
    named = jnp.zeros((EXPERTS, TOK), jnp.float32)
    weight = jnp.zeros((EXPERTS, TOK), jnp.float32)
    for k in range(TOP):
        hit = ids_ref[k : k + 1, :] == expert
        named = jnp.where(hit, 1.0, named)
        weight = jnp.where(hit, route_ref[k : k + 1, :], weight)
    before = (iota((TOK, TOK), 0) < iota((TOK, TOK), 1)).astype(jnp.float32)
    slot = jnp.dot(
        named.astype(jnp.bfloat16), before.astype(jnp.bfloat16), preferred_element_type=jnp.float32
    )
    slot = jnp.where(named > 0, slot, -1.0)
    high = weight.astype(jnp.bfloat16)
    low = (weight - high.astype(jnp.float32)).astype(jnp.bfloat16)
    lines = 8 * PEERS
    lane = iota((EXPERTS, lines), 1)
    holder = PEERS - 1 - lane // 8
    spread = (holder // 2 == iota((EXPERTS, lines), 0)).astype(jnp.float32).astype(jnp.bfloat16)

    def over_lines(table):
        return lax.dot_general(
            table, spread, (((0,), (0,)), ((), ())), preferred_element_type=jnp.float32
        )

    slots = over_lines(slot.astype(jnp.bfloat16))
    highs, lows = over_lines(high), over_lines(low)
    lane = iota((TOK, lines), 1)
    first, r = HELD * ((PEERS - 1 - lane // 8) % 2), lane % 8
    main = slots == jnp.where(r < HELD, first + r, -2).astype(jnp.float32)
    for u in range(UNITS):
        rest = slots == jnp.where(r < HELD, -2, first + 2 * u + r - HELD).astype(jnp.float32)
        for i, (hit, part) in enumerate(((main, highs), (main, lows), (rest, highs), (rest, lows))):
            out_ref[u, i * TOK : (i + 1) * TOK, :] = jnp.where(hit, part, 0.0).astype(jnp.bfloat16)


def combine_kernel(weights_ref, arrived_ref, residual_ref, out_ref):
    last = residual_ref[:, UNITS * COLS :].astype(jnp.float32)
    for u in range(UNITS):
        lines = arrived_ref[:, u].reshape(8 * PEERS, COLS)
        sums = jnp.dot(weights_ref[u], lines, preferred_element_type=jnp.float32)
        here = slice(u * COLS, (u + 1) * COLS)
        out_ref[:, here] = (
            residual_ref[:, here].astype(jnp.float32) + (sums[:TOK] + sums[TOK : 2 * TOK])
        ).astype(jnp.bfloat16)
        last = last + (sums[2 * TOK : 3 * TOK] + sums[3 * TOK :])
    out_ref[:, UNITS * COLS :] = last.astype(jnp.bfloat16)


def per_device(residual, expert_ids, route_weights, expert_out):
    width = expert_out.shape[1]
    ids, routes = expert_ids.T, route_weights.T
    in_vmem = pl.BlockSpec(memory_space=pltpu.VMEM)
    anywhere = pl.BlockSpec(memory_space=pl.ANY)
    rows = GROUP * HELD
    packed, counts = pl.pallas_call(
        pack_kernel,
        out_shape=(
            jax.ShapeDtypeStruct((PEERS, UNITS, 8, COLS), jnp.bfloat16),
            jax.ShapeDtypeStruct((8, EXPERTS), jnp.float32),
        ),
        in_specs=[anywhere, anywhere],
        out_specs=(in_vmem, in_vmem),
        scratch_shapes=[
            pltpu.VMEM(expert_out.shape, jnp.bfloat16),
            pltpu.VMEM(ids.shape, jnp.int32),
            pltpu.SemaphoreType.DMA((PEERS // GROUP,)),
            pltpu.SemaphoreType.DMA,
        ],
        compiler_params=pltpu.CompilerParams(vmem_limit_bytes=VMEM),
        name="pack",
    )(expert_out, ids)
    along_z = [[z * 16 + i for z in range(8)] for i in range(16)]
    plane = [[z * 16 + i for i in range(16)] for z in range(8)]
    gathered = lax.all_gather(counts[:1], "expert", axis=0, axis_index_groups=along_z, tiled=True)
    gathered = lax.all_gather(
        jnp.sum(gathered, axis=0, keepdims=True),
        "expert",
        axis=0,
        axis_index_groups=plane,
        tiled=True,
    )
    load = jnp.sum(gathered, axis=0)
    arrived = lax.all_to_all(
        packed.reshape(PEERS, UNITS * 8, COLS),
        "expert",
        split_axis=0,
        concat_axis=0,
        axis_index_groups=[list(range(PEERS - 1, -1, -1))],
        tiled=True,
    ).reshape(PEERS, UNITS, 8, COLS)
    weights = pl.pallas_call(
        weights_kernel,
        out_shape=jax.ShapeDtypeStruct((UNITS, 4 * TOK, 8 * PEERS), jnp.bfloat16),
        in_specs=[in_vmem, in_vmem],
        out_specs=in_vmem,
        compiler_params=pltpu.CompilerParams(vmem_limit_bytes=VMEM),
        name="weights",
    )(ids, routes)
    mixed = pl.pallas_call(
        combine_kernel,
        out_shape=jax.ShapeDtypeStruct((TOK, width), jnp.bfloat16),
        in_specs=[in_vmem, in_vmem, in_vmem],
        out_specs=in_vmem,
        compiler_params=pltpu.CompilerParams(vmem_limit_bytes=VMEM),
        name="combine",
    )(weights, arrived, residual)
    return mixed, load


def solution(mesh):
    placed = P(("dp", "expert"), None)
    return jax.shard_map(
        per_device,
        mesh=mesh,
        in_specs=(placed, placed, placed, placed),
        out_specs=(placed, P("dp")),
        check_vma=False,
    )
```

time: 86 us -> 94.8 us (1.10)
  the two profiles are of different devices: /device:TPU:6 before, /device:TPU:33 now
where the time goes in v1:
time: 94.8 us; the launch traced here: 94.5 us
  blocking collectives  66.2 us (70%)
  starting transfers between devices  15.6 us (16%)
  Pallas kernels  7 us (7%)
  local copies, waits for them, and re-layouts  3.7 us (4%)
  between operations  1.38 us (1%)
    all_gather x1, blocking collectives, per_device(): lax.all_gather(counts[:1], 'expert', axis=0, axis_index_groups=along_z, t...  40.1 us
    unnamed x1, blocking collectives  26.1 us
    all_to_all x1, starting transfers between devices, per_device(): lax.all_to_all(packed.reshape(PEERS, UNITS * 8, COLS), 'expert', split_ax...  15.6 us
    pallas_call x1, Pallas kernels, per_device(): pl.pallas_call(pack_kernel, out_shape=(jax.ShapeDtypeStruct((PEERS, UNITS...  5.23 us
    unnamed x14, local copies, waits for them, and re-layouts  3.63 us
  transfers between devices with their start and end apart: 1, of which 0 were waited for; matrix products, arithmetic and copies ran while one was open for 2% of the time, Pallas kernels for 1%

profile of v1, /device:TPU:33, one launch (start us, length us, event | category | flops | bytes accessed | tf_op | source)
XLA Modules:
  0.0 94.5 jit_solution(8732558062377795703)
XLA Ops:
  0.6 0.0 copy-start
  0.6 1.4 %copy-done = bf16[768,1024]{1,0:T(8,128)(2,1)S(1)} copy-done((bf16[768,1024]{1,0:T(8,128)(2,1)S(1)}, bf16[768,1024]{1,0:T(8,128)(2,1)}, u32[]{:S(2)}) %copy-start) | copy-done | bytes 1572888
  2.0 0.0 copy-start.2
  2.0 0.7 copy-done.2
  2.7 5.2 %pack.1 = (bf16[128,3,8,256]{3,2,1,0:T(8,128)(2,1)}, f32[8,64]{1,0:T(8,128)S(1)}) custom-call(bf16[768,1024]{1,0:T(8,128)(2,1)S(1)} %copy-done, s32[8,64]{1,0:T(8,128)S(1)} %bitcast.8), custom_call_target="tpu_custom_call" | custom-call | tf_op jit(solution)/shard_map/pack/pallas_call | solution.py:120
  8.0 0.0 copy-start.3
  8.0 0.0 copy-start.4
  8.0 15.6 %all-to-all-start = ((bf16[128,24,256]{2,1,0:T(8,128)(2,1)}), bf16[128,24,256]{2,1,0:T(8,128)(2,1)S(1)}, u32[]{:S(2)}, u32[]{:S(2)}) async-start(bf16[128,24,256]{2,1,0:T(8,128)(2,1)} %bitcast.2), calls=%async_computation | async-start | bytes 3145728 | tf_op jit(solution)/shard_map/all_to_all | solution.py:148
  23.6 0.0 copy-start.1
  23.6 0.0 copy-done.3
  23.6 0.0 copy-done.4
  23.7 0.5 weights.1.weights_ref
  24.2 40.1 %all-gather.1 = f32[8,1,64]{2,1,0:T(1,128)S(1)} all-gather(f32[1,1,64]{2,1,0:T(1,128)S(1)} %slice_bitcast_fusion), channel_id=1, replica_groups={{0,16,32,48,64,80,96,112},{1,17,33,49,65,81,97,113},{2,18,34,50,66,82,9..., dimensions={0}, use_global_device_ids=true | all-gather | bytes 2304 | tf_op jit(solution)/shard_map/all_gather | solution.py:139
  64.4 1.3 %dynamic-slice = u32[1]{0:T(128)} dynamic-slice(u32[512]{0:T(512)} %constant.8, u32[]{:T(128)S(6)} %add), dynamic_slice_sizes={1} | dynamic-slice | bytes 12
  66.3 0.2 dynamic-update-slice
  66.5 26.1 %all-reduce = f32[1024]{0:T(1024)S(1)} all-reduce(f32[1024]{0:T(1024)S(1)} %dynamic-update-slice), channel_id=2, replica_groups={{0,1,2,3,4,5,6,7,8,9,10,11,12,13,14,15},{16,17,18,19,20,21,22,23,24,25,..., use_global_device_ids=true, to_apply=%add | all-reduce | flops 1024 | bytes 8192
  92.6 0.1 reshape.12
  92.7 0.5 reduce_sum.19
  93.2 0.0 all-to-all-done
  93.2 0.0 copy-done.1
  93.3 1.2 %combine.1 = bf16[64,1024]{1,0:T(8,128)(2,1)} custom-call(bf16[3,256,1024]{2,1,0:T(8,128)(2,1)S(1)} %weights.1.weights_ref, bf16[128,3,8,256]{3,2,1,0:T(8,128)(2,1)S(1)} %bitcast.7, bf16[64,1024]{1,0:T(8,128)(2,1)S(1)} %copy-done.1), custom_call_target="tpu_custom_call" | custom-call | tf_op jit(solution)/shard_map/combine/pallas_call | solution.py:164
  (3 shorter events, 0.0 us)
Async XLA Ops:
  0.6 1.4 %copy-start = (bf16[768,1024]{1,0:T(8,128)(2,1)S(1)}, bf16[768,1024]{1,0:T(8,128)(2,1)}, u32[]{:S(2)}) copy-start(bf16[768,1024]{1,0:T(8,128)(2,1)} %x_hbm.1) | copy-start | bytes 4718596
  2.0 0.7 copy-start.2
  8.0 15.7 %copy-start.3 = (s32[64,8]{0,1:T(8,128)S(1)}, s32[64,8]{0,1:T(8,128)}, u32[]{:S(2)}) copy-start(s32[64,8]{0,1:T(8,128)} %param.5) | copy-start | bytes 6148
  8.0 15.7 %copy-start.4 = (f32[64,8]{0,1:T(8,128)S(1)}, f32[64,8]{0,1:T(8,128)}, u32[]{:S(2)}) copy-start(f32[64,8]{0,1:T(8,128)} %param.6) | copy-start | bytes 6148
  8.0 85.3 %all-to-all-start = ((bf16[128,24,256]{2,1,0:T(8,128)(2,1)}), bf16[128,24,256]{2,1,0:T(8,128)(2,1)S(1)}, u32[]{:S(2)}, u32[]{:S(2)}) async-start(bf16[128,24,256]{2,1,0:T(8,128)(2,1)} %bitcast.2), calls=%async_computation | async-start | bytes 3145728 | tf_op jit(solution)/shard_map/all_to_all | solution.py:148
  23.6 69.6 %copy-start.1 = (bf16[64,1024]{1,0:T(8,128)(2,1)S(1)}, bf16[64,1024]{1,0:T(8,128)(2,1)}, u32[]{:S(2)}) copy-start(bf16[64,1024]{1,0:T(8,128)(2,1)} %residual_ref.1) | copy-start | bytes 393220

commit v2 on v1

v2 whole, which is shorter than its diff:
```python
import jax
import jax.numpy as jnp
from jax import lax
from jax.experimental import pallas as pl
from jax.experimental.pallas import tpu as pltpu
from jax.sharding import PartitionSpec as P

EXPERTS = 64
TOP = 8
TOK = 64
HELD = 6
PEERS = 128
LANES = 128
LINES = 50
QUAD = 4
TILES = QUAD * LINES // 8
OCT = 8
DATA = OCT * HELD * 8

FIRST = (0, 6, 13, 19)


def iota(shape, dim):
    return lax.broadcasted_iota(jnp.int32, shape, dim)


def as_bf16(mask):
    return mask.astype(jnp.float32).astype(jnp.bfloat16)


def pack_kernel(x_hbm, ids_hbm, out_hbm, x_ref, ids_ref, out_ref, x_sems, ids_sem, out_sems):
    rows = 2 * OCT * HELD
    steps = PEERS // (2 * OCT)
    x_copies, out_copies = [], []
    for g in range(steps):
        here = pl.ds(g * rows, rows)
        there = pl.ds((steps - 1 - g) * 2 * OCT * LINES, 2 * OCT * LINES)
        x_copies.append(pltpu.make_async_copy(x_hbm.at[here], x_ref.at[here], x_sems.at[g]))
        out_copies.append(
            pltpu.make_async_copy(out_ref.at[there], out_hbm.at[there], out_sems.at[g])
        )
    ids_copy = pltpu.make_async_copy(ids_hbm, ids_ref, ids_sem)
    ids_copy.start()
    for copy in x_copies:
        copy.start()
    block = (PEERS - 1 - lax.axis_index("expert")) % QUAD
    line = iota((OCT * LINES, LANES), 0)
    owner = line * 0
    for b in range(1, OCT):
        owner = jnp.where(line >= b * LINES, b, owner)
    place = line - owner * LINES + block * LINES
    t, r = place >> 3, place & 7
    c = t - jnp.where(t < 6, 0, jnp.where(t < 12, 6, jnp.where(t < 19, 13, 19)))
    main = jnp.where(t == 6, r - 2, r)
    rest = jnp.where(t == 12, jnp.where(r < 2, 0, 5), c)
    rest_row = 2 * jnp.where(rest >= 3, rest - 3, rest) + jnp.where(r < 2, r, r - 6)
    source = jnp.where((t != 12) & (main >= 0) & (main < HELD), OCT * HELD * c + main, 0)
    is_rest = ((t == 12) & (r < 2)) | ((t != 6) & (t != 18) & (r >= 6))
    source = jnp.where(
        is_rest, OCT * HELD * jnp.where(rest >= 3, 7, 6) + rest_row, source
    )
    source = source + HELD * (OCT - 1 - owner)
    tally = ((t == 6) & (r < 2)) | ((t == 12) & (r >= 2) & (r < 6)) | ((t == 18) & (r >= 6))
    source = jnp.where(tally, jnp.where((r & 1) == 0, DATA, -1), source)
    column = iota((OCT * LINES, LANES), 1)
    tails = (LANES, LANES, LANES, 16)
    pick = jnp.concatenate(
        [as_bf16(source == column + i * LANES)[:, :n] for i, n in enumerate(tails)], axis=1
    )
    ids_copy.wait()
    expert = iota((LANES, TOK), 0)
    named = jnp.zeros((LANES, TOK), jnp.float32)
    for k in range(TOP):
        named = named + (ids_ref[k : k + 1, :] == expert).astype(jnp.float32)
    counts = lax.dot_general(
        jnp.ones((16, TOK), jnp.bfloat16),
        named.astype(jnp.bfloat16),
        (((1,), (1,)), ((), ())),
        preferred_element_type=jnp.float32,
    ).astype(jnp.bfloat16)
    counts = jnp.concatenate([counts, counts], axis=1)
    for copy in x_copies:
        copy.wait()
    for g in range(steps):
        one = x_ref[pl.ds(g * rows, rows // 2), :]
        two = x_ref[pl.ds(g * rows + rows // 2, rows // 2), :]
        stack = [
            jnp.concatenate(
                [one[:, i * LANES : (i + 1) * LANES], two[:, i * LANES : (i + 1) * LANES]], axis=1
            )
            for i in range(8)
        ]
        packed = jnp.dot(
            pick, jnp.concatenate(stack + [counts], axis=0), preferred_element_type=jnp.float32
        ).astype(jnp.bfloat16)
        start = (steps - 1 - g) * 2 * OCT * LINES
        out_ref[pl.ds(start + OCT * LINES, OCT * LINES), :] = packed[:, :LANES]
        out_ref[pl.ds(start, OCT * LINES), :] = packed[:, LANES:]
        if g % 2:
            out_copies[g - 1].start()
            out_copies[g].start()
    for copy in out_copies:
        copy.wait()


def weights_kernel(ids_ref, route_ref, out_ref, odd_ref):
    expert = iota((EXPERTS, TOK), 0)
    named = jnp.zeros((EXPERTS, TOK), jnp.float32)
    weight = jnp.zeros((EXPERTS, TOK), jnp.float32)
    for k in range(TOP):
        hit = ids_ref[k : k + 1, :] == expert
        named = jnp.where(hit, 1.0, named)
        weight = jnp.where(hit, route_ref[k : k + 1, :], weight)
    before = as_bf16(iota((TOK, TOK), 0) < iota((TOK, TOK), 1))
    slot = jnp.dot(named.astype(jnp.bfloat16), before, preferred_element_type=jnp.float32)
    slot = jnp.where(named > 0, slot, -1.0)
    high = weight.astype(jnp.bfloat16)
    low = (weight - high.astype(jnp.float32)).astype(jnp.bfloat16)
    width = 8 * PEERS
    per_block = width // QUAD

    def holder_of(line):
        return PEERS - 1 - (QUAD * ((line % per_block) // 8) + line // per_block)

    spread = as_bf16(
        holder_of(iota((EXPERTS, width), 1)) // 2 == iota((EXPERTS, width), 0)
    )

    def over_lines(table):
        return lax.dot_general(
            table, spread, (((0,), (0,)), ((), ())), preferred_element_type=jnp.float32
        )

    slots = over_lines(slot.astype(jnp.bfloat16))
    highs, lows = over_lines(high), over_lines(low)
    line = iota((TOK, width), 1)
    q, r = line // per_block, line % 8
    first = HELD * (holder_of(line) % 2)
    slots = slots - first.astype(jnp.float32)

    def hits(wanted):
        return (slots == wanted.astype(jnp.float32)) & (wanted >= 0)

    main = jnp.where(r < HELD, r, -1)
    rests = [jnp.where(r < HELD, -1, 2 * i + r - HELD) for i in range(3)]
    for j, wanted in enumerate([main] + rests):
        hit = hits(wanted)
        for i, part in enumerate((highs, lows)):
            out_ref[j, i * TOK : (i + 1) * TOK, :] = jnp.where(hit, part, 0.0).astype(jnp.bfloat16)
    odd = hits(jnp.where(q == 1, r - 2, -1))
    shared = hits(
        jnp.where((q == 1) & (r < 2), r, jnp.where((q == 2) & (r >= 6), r - 2, -1))
    )
    wanted = ((odd, 1, highs), (odd, 1, lows))
    wanted += ((shared, 1, highs), (shared, 1, lows), (shared, 2, highs), (shared, 2, lows))
    for i, (hit, b, part) in enumerate(wanted):
        odd_ref[i * TOK : (i + 1) * TOK, :] = jnp.where(hit, part, 0.0)[
            :, b * per_block : (b + 1) * per_block
        ].astype(jnp.bfloat16)


def combine_kernel(weights_ref, odd_ref, arrived_ref, residual_ref, out_ref, load_ref):
    quads = PEERS // QUAD
    per_block = 8 * quads

    def table(j, b=None, part=None):
        whole = weights_ref[j]
        if b is None:
            return whole
        return jnp.concatenate(
            [whole[:, : b * per_block], part, whole[:, (b + 1) * per_block :]], axis=1
        )


    def tile(t):
        return arrived_ref[:, t].reshape(8 * quads, LANES)

    def columns(c):
        return slice(c * LANES, (c + 1) * LANES)

    r = iota((8, 8 * quads), 1) % 8
    load = jnp.zeros((8, LANES), jnp.float32)
    for t, wanted in ((6, r == 0), (12, (r == 2) | (r == 4)), (18, r == 6)):
        load = load + jnp.dot(as_bf16(wanted), tile(t), preferred_element_type=jnp.float32)
    load_ref[...] = load[:1, :EXPERTS]
    sums = jnp.dot(odd_ref[2 * TOK :], tile(12), preferred_element_type=jnp.float32)
    none = jnp.zeros((2 * TOK, per_block), jnp.bfloat16)
    tails = [
        residual_ref[:, columns(6 + i)].astype(jnp.float32)
        + (sums[2 * i * TOK : (2 * i + 1) * TOK] + sums[(2 * i + 1) * TOK : (2 * i + 2) * TOK])
        for i in range(2)
    ]
    for c in range(6):
        lines = jnp.concatenate([tile(f + c) for f in FIRST], axis=0)
        main = table(0, 1, odd_ref[: 2 * TOK]) if c == 0 else table(0)
        rest = table(1 + c % 3, {0: 1, 5: 2}.get(c), none)
        sums = jnp.dot(
            jnp.concatenate([main, rest], axis=0), lines, preferred_element_type=jnp.float32
        )
        out_ref[:, columns(c)] = (
            residual_ref[:, columns(c)].astype(jnp.float32) + (sums[:TOK] + sums[TOK : 2 * TOK])
        ).astype(jnp.bfloat16)
        tails[c // 3] = tails[c // 3] + (sums[2 * TOK : 3 * TOK] + sums[3 * TOK :])
    for i in range(2):
        out_ref[:, columns(6 + i)] = tails[i].astype(jnp.bfloat16)


def per_device(residual, expert_ids, route_weights, expert_out):
    width = expert_out.shape[1]
    ids, routes = expert_ids.T, route_weights.T
    in_vmem = pl.BlockSpec(memory_space=pltpu.VMEM)
    in_hbm = pl.BlockSpec(memory_space=pltpu.HBM)
    steps = PEERS // (2 * OCT)
    packed = pl.pallas_call(
        pack_kernel,
        out_shape=jax.ShapeDtypeStruct((PEERS * LINES, LANES), jnp.bfloat16),
        in_specs=[in_hbm, in_hbm],
        out_specs=in_hbm,
        scratch_shapes=[
            pltpu.VMEM(expert_out.shape, jnp.bfloat16),
            pltpu.VMEM(ids.shape, jnp.int32),
            pltpu.VMEM((PEERS * LINES, LANES), jnp.bfloat16),
            pltpu.SemaphoreType.DMA((steps,)),
            pltpu.SemaphoreType.DMA,
            pltpu.SemaphoreType.DMA((steps,)),
        ],
        compiler_params=pltpu.CompilerParams(vmem_limit_bytes=60 * 2**20),
        name="pack",
    )(expert_out, ids)
    arrived = lax.all_to_all(
        packed.reshape(PEERS, LINES // 2, 2, LANES),
        "expert",
        split_axis=0,
        concat_axis=0,
        axis_index_groups=[list(range(PEERS - 1, -1, -1))],
        tiled=True,
    ).reshape(PEERS // QUAD, TILES, 8, LANES)
    weights, odd = pl.pallas_call(
        weights_kernel,
        out_shape=(
            jax.ShapeDtypeStruct((4, 2 * TOK, 8 * PEERS), jnp.bfloat16),
            jax.ShapeDtypeStruct((6 * TOK, 8 * PEERS // QUAD), jnp.bfloat16),
        ),
        in_specs=[in_vmem, in_vmem],
        out_specs=(in_vmem, in_vmem),
        compiler_params=pltpu.CompilerParams(vmem_limit_bytes=24 * 2**20),
        name="weights",
    )(ids, routes)
    mixed, load = pl.pallas_call(
        combine_kernel,
        out_shape=(
            jax.ShapeDtypeStruct((TOK, width), jnp.bfloat16),
            jax.ShapeDtypeStruct((1, EXPERTS), jnp.float32),
        ),
        in_specs=[in_vmem, in_vmem, in_vmem, in_vmem],
        out_specs=(in_vmem, in_vmem),
        compiler_params=pltpu.CompilerParams(vmem_limit_bytes=24 * 2**20),
        name="combine",
    )(weights, odd, arrived, residual)
    return mixed, load.reshape(EXPERTS)


def solution(mesh):
    placed = P(("dp", "expert"), None)
    return jax.shard_map(
        per_device,
        mesh=mesh,
        in_specs=(placed, placed, placed, placed),
        out_specs=(placed, P("dp")),
        check_vma=False,
    )
```

time: 94.8 us -> 64 us (0.68)
  the two profiles are of different devices: /device:TPU:33 before, /device:TPU:6 now
where the time goes in v2:
time: 64 us; the launch traced here: 63.8 us
  waiting for transfers between devices  39.2 us (61%)
  starting transfers between devices  18.1 us (28%)
  Pallas kernels  5.79 us (9%)
  between operations  0.69 us (1%)
    all_to_all x1, waiting for transfers between devices, per_device(): lax.all_to_all(packed.reshape(PEERS, LINES // 2, 2, LANES), 'expert', spl...  39.2 us
    all_to_all x1, starting transfers between devices, per_device(): lax.all_to_all(packed.reshape(PEERS, LINES // 2, 2, LANES), 'expert', spl...  18.1 us
    pallas_call x1, Pallas kernels, per_device(): pl.pallas_call(pack_kernel, out_shape=jax.ShapeDtypeStruct((PEERS * LINES...  3.43 us
    pallas_call x1, Pallas kernels, per_device(): pl.pallas_call(combine_kernel, out_shape=(jax.ShapeDtypeStruct((TOK, widt...  1.67 us
  transfers between devices with their start and end apart: 1, of which 1 were waited for; matrix products, arithmetic and copies ran while one was open for 0% of the time, Pallas kernels for 1%

profile of v2, /device:TPU:6, one launch (start us, length us, event | category | flops | bytes accessed | tf_op | source)
XLA Modules:
  0.0 63.8 jit_solution(14810598751971777031)
XLA Ops:
  0.6 3.4 %pack.1 = bf16[6400,128]{1,0:T(8,128)(2,1)} custom-call(bf16[768,1024]{1,0:T(8,128)(2,1)} %x_hbm.1, s32[8,64]{1,0:T(8,128)} %bitcast.6), custom_call_target="tpu_custom_call" | custom-call | tf_op jit(solution)/shard_map/pack/pallas_call | solution.py:214
  4.1 0.0 copy-start.1
  4.1 0.0 copy-start.2
  4.1 0.0 copy-start
  4.1 18.1 %all-to-all-start = ((bf16[128,25,2,128]{3,2,1,0:T(2,128)(2,1)}), bf16[128,25,2,128]{3,2,1,0:T(2,128)(2,1)S(1)}, u32[]{:S(2)}, u32[]{:S(2)}) async-start(bf16[128,25,2,128]{3,2,1,0:T(2,128)(2,1)} %bitcast.9), calls=%async_computation | async-start | bytes 3276800 | tf_op jit(solution)/shard_map/all_to_all | solution.py:230
  22.2 0.0 copy-done.1
  22.2 0.0 copy-done.2
  22.2 0.7 %weights.1 = (bf16[4,128,1024]{2,1,0:T(8,128)(2,1)S(1)}, bf16[384,256]{1,0:T(8,128)(2,1)S(1)}) custom-call(s32[8,64]{1,0:T(8,128)S(1)} %bitcast.7, f32[8,64]{1,0:T(8,128)S(1)} %bitcast.8), custom_call_target="tpu_custom_call" | custom-call | tf_op jit(solution)/shard_map/weights/pallas_call | solution.py:238
  22.9 39.2 %all-to-all-done = bf16[128,25,2,128]{3,2,1,0:T(2,128)(2,1)S(1)} async-done(((bf16[128,25,2,128]{3,2,1,0:T(2,128)(2,1)}), bf16[128,25,2,128]{3,2,1,0:T(2,128)(2,1)S(1)}, u32[]{:S(2)}, u32[]{:S(2)}) %all-to-all-start) | async-done | bytes 1638432 | tf_op jit(solution)/shard_map/all_to_all | solution.py:230
  62.1 0.0 copy-done
  62.1 1.7 %combine.1 = (bf16[64,1024]{1,0:T(8,128)(2,1)}, f32[1,64]{1,0:T(1,128)}) custom-call(bf16[4,128,1024]{2,1,0:T(8,128)(2,1)S(1)} %get-tuple-element.6.weights_ref, bf16[384,256]{1,0:T(8,128)(2,1)S(1)} %get-tuple-element.7.odd_ref, bf16[32,25,8,128]{3,2,1,0:T(8,128)(2,1)S(1)} %bitcast.5, bf16[64,1024]{1,0:T(8,128)(2,1)S(1)} %copy-done), custom_call_target="tpu_custom_call" | custom-call | tf_op jit(solution)/shard_map/combine/pallas_call | solution.py:249
Async XLA Ops:
  4.1 18.2 %copy-start.1 = (s32[64,8]{0,1:T(8,128)S(1)}, s32[64,8]{0,1:T(8,128)}, u32[]{:S(2)}) copy-start(s32[64,8]{0,1:T(8,128)} %param.5) | copy-start | bytes 6148
  4.1 18.2 %copy-start.2 = (f32[64,8]{0,1:T(8,128)S(1)}, f32[64,8]{0,1:T(8,128)}, u32[]{:S(2)}) copy-start(f32[64,8]{0,1:T(8,128)} %param.6) | copy-start | bytes 6148
  4.1 58.1 %copy-start = (bf16[64,1024]{1,0:T(8,128)(2,1)S(1)}, bf16[64,1024]{1,0:T(8,128)(2,1)}, u32[]{:S(2)}) copy-start(bf16[64,1024]{1,0:T(8,128)(2,1)} %residual_ref.1) | copy-start | bytes 393220
  4.1 58.0 %all-to-all-start = ((bf16[128,25,2,128]{3,2,1,0:T(2,128)(2,1)}), bf16[128,25,2,128]{3,2,1,0:T(2,128)(2,1)S(1)}, u32[]{:S(2)}, u32[]{:S(2)}) async-start(bf16[128,25,2,128]{3,2,1,0:T(2,128)(2,1)} %bitcast.9), calls=%async_computation | async-start | bytes 3276800 | tf_op jit(solution)/shard_map/all_to_all | solution.py:230

commit v3 on v2

--- a/solution.py
+++ b/solution.py
@@ -15,7 +15,7 @@
 QUAD = 4
 TILES = QUAD * LINES // 8
 OCT = 8
-DATA = OCT * HELD * 8
+STACK = 32
 
 FIRST = (0, 6, 13, 19)
 
@@ -44,9 +44,9 @@
     for copy in x_copies:
         copy.start()
     block = (PEERS - 1 - lax.axis_index("expert")) % QUAD
-    line = iota((OCT * LINES, LANES), 0)
+    line = iota((QUAD * LINES, LANES), 0)
     owner = line * 0
-    for b in range(1, OCT):
+    for b in range(1, QUAD):
         owner = jnp.where(line >= b * LINES, b, owner)
     place = line - owner * LINES + block * LINES
     t, r = place >> 3, place & 7
@@ -54,19 +54,19 @@
     main = jnp.where(t == 6, r - 2, r)
     rest = jnp.where(t == 12, jnp.where(r < 2, 0, 5), c)
     rest_row = 2 * jnp.where(rest >= 3, rest - 3, rest) + jnp.where(r < 2, r, r - 6)
-    source = jnp.where((t != 12) & (main >= 0) & (main < HELD), OCT * HELD * c + main, 0)
-    is_rest = ((t == 12) & (r < 2)) | ((t != 6) & (t != 18) & (r >= 6))
-    source = jnp.where(
-        is_rest, OCT * HELD * jnp.where(rest >= 3, 7, 6) + rest_row, source
-    )
-    source = source + HELD * (OCT - 1 - owner)
+    source = jnp.where((t != 12) & (main >= 0) & (main < HELD), STACK * c + main, 0)
+    is_rest = ((t == 12) & ((r < 2) | (r >= 6))) | ((t != 6) & (t != 12) & (t != 18) & (r >= 6))
+    source = jnp.where(is_rest, STACK * jnp.where(rest >= 3, 7, 6) + rest_row, source)
+    source = source + HELD * (QUAD - 1 - owner)
     tally = ((t == 6) & (r < 2)) | ((t == 12) & (r >= 2) & (r < 6)) | ((t == 18) & (r >= 6))
-    source = jnp.where(tally, jnp.where((r & 1) == 0, DATA, -1), source)
-    column = iota((OCT * LINES, LANES), 1)
-    tails = (LANES, LANES, LANES, 16)
-    pick = jnp.concatenate(
-        [as_bf16(source == column + i * LANES)[:, :n] for i, n in enumerate(tails)], axis=1
-    )
+    blank = (r & 1) == 1
+    column = iota((QUAD * LINES, LANES), 1)
+    picks = []
+    for spare, shift in ((STACK - 8, 0), (0, 8)):
+        here = jnp.where(tally, jnp.where(blank, -1, spare), source + shift)
+        picks.append(
+            jnp.concatenate([as_bf16(here == column), as_bf16(here == column + LANES)], axis=1)
+        )
     ids_copy.wait()
     expert = iota((LANES, TOK), 0)
     named = jnp.zeros((LANES, TOK), jnp.float32)
@@ -77,22 +77,35 @@
         named.astype(jnp.bfloat16),
         (((1,), (1,)), ((), ())),
         preferred_element_type=jnp.float32,
-    ).astype(jnp.bfloat16)
+    )
     counts = jnp.concatenate([counts, counts], axis=1)
+    upper = iota((16, 2 * LANES), 0) < 8
     for copy in x_copies:
         copy.wait()
     for g in range(steps):
         one = x_ref[pl.ds(g * rows, rows // 2), :]
         two = x_ref[pl.ds(g * rows + rows // 2, rows // 2), :]
-        stack = [
-            jnp.concatenate(
-                [one[:, i * LANES : (i + 1) * LANES], two[:, i * LANES : (i + 1) * LANES]], axis=1
+        thirds = []
+        for i in range(8):
+            here = slice(i * LANES, (i + 1) * LANES)
+            both = jnp.concatenate([one[:, here], two[:, here]], axis=1)
+            thirds.append((both[:16], both[16:32], both[32:]))
+        middle = thirds[0][1].astype(jnp.float32)
+        spare = (
+            jnp.where(upper, middle, counts).astype(jnp.bfloat16),
+            jnp.where(upper, counts, middle).astype(jnp.bfloat16),
+        )
+        packed = []
+        for half in range(2):
+            stack = [thirds[0][0], spare[0]] if half == 0 else [spare[1], thirds[0][2]]
+            for i in range(1, 8):
+                stack += thirds[i][half : half + 2]
+            packed.append(
+                jnp.dot(
+                    picks[half], jnp.concatenate(stack, axis=0), preferred_element_type=jnp.float32
+                )
             )
-            for i in range(8)
-        ]
-        packed = jnp.dot(
-            pick, jnp.concatenate(stack + [counts], axis=0), preferred_element_type=jnp.float32
-        ).astype(jnp.bfloat16)
+        packed = jnp.concatenate(packed[::-1], axis=0).astype(jnp.bfloat16)
         start = (steps - 1 - g) * 2 * OCT * LINES
         out_ref[pl.ds(start + OCT * LINES, OCT * LINES), :] = packed[:, :LANES]
         out_ref[pl.ds(start, OCT * LINES), :] = packed[:, LANES:]
@@ -163,15 +176,6 @@
     quads = PEERS // QUAD
     per_block = 8 * quads
 
-    def table(j, b=None, part=None):
-        whole = weights_ref[j]
-        if b is None:
-            return whole
-        return jnp.concatenate(
-            [whole[:, : b * per_block], part, whole[:, (b + 1) * per_block :]], axis=1
-        )
-
-
     def tile(t):
         return arrived_ref[:, t].reshape(8 * quads, LANES)
 
@@ -184,23 +188,45 @@
         load = load + jnp.dot(as_bf16(wanted), tile(t), preferred_element_type=jnp.float32)
     load_ref[...] = load[:1, :EXPERTS]
     sums = jnp.dot(odd_ref[2 * TOK :], tile(12), preferred_element_type=jnp.float32)
-    none = jnp.zeros((2 * TOK, per_block), jnp.bfloat16)
     tails = [
         residual_ref[:, columns(6 + i)].astype(jnp.float32)
         + (sums[2 * i * TOK : (2 * i + 1) * TOK] + sums[(2 * i + 1) * TOK : (2 * i + 2) * TOK])
         for i in range(2)
     ]
-    for c in range(6):
-        lines = jnp.concatenate([tile(f + c) for f in FIRST], axis=0)
-        main = table(0, 1, odd_ref[: 2 * TOK]) if c == 0 else table(0)
-        rest = table(1 + c % 3, {0: 1, 5: 2}.get(c), none)
+    none = jnp.zeros((per_block, LANES), jnp.bfloat16)
+    odd = {
+        0: jnp.dot(odd_ref[: 2 * TOK], tile(6), preferred_element_type=jnp.float32),
+        5: jnp.dot(
+            weights_ref[0, :, 2 * per_block : 3 * per_block],
+            tile(18),
+            preferred_element_type=jnp.float32,
+        ),
+    }
+    for c in range(3):
+        lines = jnp.concatenate(
+            [
+                jnp.concatenate(
+                    [none if f + i in (6, 18) else tile(f + i) for i in (c, c + 3)], axis=1
+                )
+                for f in FIRST
+            ],
+            axis=0,
+        )
         sums = jnp.dot(
-            jnp.concatenate([main, rest], axis=0), lines, preferred_element_type=jnp.float32
-        )
-        out_ref[:, columns(c)] = (
-            residual_ref[:, columns(c)].astype(jnp.float32) + (sums[:TOK] + sums[TOK : 2 * TOK])
-        ).astype(jnp.bfloat16)
-        tails[c // 3] = tails[c // 3] + (sums[2 * TOK : 3 * TOK] + sums[3 * TOK :])
+            jnp.concatenate([weights_ref[0], weights_ref[1 + c]], axis=0),
+            lines,
+            preferred_element_type=jnp.float32,
+        )
+        for i in range(2):
+            part = sums[:, columns(i)]
+            main = part[:TOK] + part[TOK : 2 * TOK]
+            if c + 3 * i in odd:
+                main = main + (odd[c + 3 * i][:TOK] + odd[c + 3 * i][TOK:])
+            here = columns(c + 3 * i)
+            out_ref[:, here] = (residual_ref[:, here].astype(jnp.float32) + main).astype(
+                jnp.bfloat16
+            )
+            tails[i] = tails[i] + (part[2 * TOK : 3 * TOK] + part[3 * TOK :])
     for i in range(2):
         out_ref[:, columns(6 + i)] = tails[i].astype(jnp.bfloat16)
 

time: 64 us -> 63.3 us (0.989)
  Pallas kernels: 5.79 us -> 5.09 us
where the time goes in v3:
time: 63.3 us; the launch traced here: 63.1 us
  waiting for transfers between devices  39.2 us (62%)
  starting transfers between devices  18.1 us (29%)
  Pallas kernels  5.09 us (8%)
  between operations  0.69 us (1%)
    all_to_all x1, waiting for transfers between devices, per_device(): lax.all_to_all(packed.reshape(PEERS, LINES // 2, 2, LANES), 'expert', spl...  39.2 us
    all_to_all x1, starting transfers between devices, per_device(): lax.all_to_all(packed.reshape(PEERS, LINES // 2, 2, LANES), 'expert', spl...  18.1 us
    pallas_call x1, Pallas kernels, per_device(): pl.pallas_call(pack_kernel, out_shape=jax.ShapeDtypeStruct((PEERS * LINES...  3.12 us
    pallas_call x1, Pallas kernels, per_device(): pl.pallas_call(combine_kernel, out_shape=(jax.ShapeDtypeStruct((TOK, widt...  1.29 us
  transfers between devices with their start and end apart: 1, of which 1 were waited for; matrix products, arithmetic and copies ran while one was open for 0% of the time, Pallas kernels for 1%

profile of v3, /device:TPU:6, one launch (start us, length us, event | category | flops | bytes accessed | tf_op | source)
XLA Modules:
  0.0 63.1 jit_solution(2936932029258775565)
XLA Ops:
  0.6 3.1 %pack.1 = bf16[6400,128]{1,0:T(8,128)(2,1)} custom-call(bf16[768,1024]{1,0:T(8,128)(2,1)} %x_hbm.1, s32[8,64]{1,0:T(8,128)} %bitcast.6), custom_call_target="tpu_custom_call" | custom-call | tf_op jit(solution)/shard_map/pack/pallas_call | solution.py:240
  3.8 0.0 copy-start.1
  3.8 0.0 copy-start.2
  3.8 0.0 copy-start
  3.8 18.1 %all-to-all-start = ((bf16[128,25,2,128]{3,2,1,0:T(2,128)(2,1)}), bf16[128,25,2,128]{3,2,1,0:T(2,128)(2,1)S(1)}, u32[]{:S(2)}, u32[]{:S(2)}) async-start(bf16[128,25,2,128]{3,2,1,0:T(2,128)(2,1)} %bitcast.9), calls=%async_computation | async-start | bytes 3276800 | tf_op jit(solution)/shard_map/all_to_all | solution.py:256
  21.9 0.0 copy-done.1
  21.9 0.0 copy-done.2
  21.9 0.7 %weights.1 = (bf16[4,128,1024]{2,1,0:T(8,128)(2,1)S(1)}, bf16[384,256]{1,0:T(8,128)(2,1)S(1)}) custom-call(s32[8,64]{1,0:T(8,128)S(1)} %bitcast.7, f32[8,64]{1,0:T(8,128)S(1)} %bitcast.8), custom_call_target="tpu_custom_call" | custom-call | tf_op jit(solution)/shard_map/weights/pallas_call | solution.py:264
  22.6 39.2 %all-to-all-done = bf16[128,25,2,128]{3,2,1,0:T(2,128)(2,1)S(1)} async-done(((bf16[128,25,2,128]{3,2,1,0:T(2,128)(2,1)}), bf16[128,25,2,128]{3,2,1,0:T(2,128)(2,1)S(1)}, u32[]{:S(2)}, u32[]{:S(2)}) %all-to-all-start) | async-done | bytes 1638432 | tf_op jit(solution)/shard_map/all_to_all | solution.py:256
  61.8 0.0 copy-done
  61.8 1.3 %combine.1 = (bf16[64,1024]{1,0:T(8,128)(2,1)}, f32[1,64]{1,0:T(1,128)}) custom-call(bf16[4,128,1024]{2,1,0:T(8,128)(2,1)S(1)} %get-tuple-element.6.weights_ref, bf16[384,256]{1,0:T(8,128)(2,1)S(1)} %get-tuple-element.7.odd_ref, bf16[32,25,8,128]{3,2,1,0:T(8,128)(2,1)S(1)} %bitcast.5, bf16[64,1024]{1,0:T(8,128)(2,1)S(1)} %copy-done), custom_call_target="tpu_custom_call" | custom-call | tf_op jit(solution)/shard_map/combine/pallas_call | solution.py:275
Async XLA Ops:
  3.8 18.2 %copy-start.1 = (s32[64,8]{0,1:T(8,128)S(1)}, s32[64,8]{0,1:T(8,128)}, u32[]{:S(2)}) copy-start(s32[64,8]{0,1:T(8,128)} %param.5) | copy-start | bytes 6148
  3.8 18.2 %copy-start.2 = (f32[64,8]{0,1:T(8,128)S(1)}, f32[64,8]{0,1:T(8,128)}, u32[]{:S(2)}) copy-start(f32[64,8]{0,1:T(8,128)} %param.6) | copy-start | bytes 6148
  3.8 58.1 %copy-start = (bf16[64,1024]{1,0:T(8,128)(2,1)S(1)}, bf16[64,1024]{1,0:T(8,128)(2,1)}, u32[]{:S(2)}) copy-start(bf16[64,1024]{1,0:T(8,128)(2,1)} %residual_ref.1) | copy-start | bytes 393220
  3.8 58.0 %all-to-all-start = ((bf16[128,25,2,128]{3,2,1,0:T(2,128)(2,1)}), bf16[128,25,2,128]{3,2,1,0:T(2,128)(2,1)S(1)}, u32[]{:S(2)}, u32[]{:S(2)}) async-start(bf16[128,25,2,128]{3,2,1,0:T(2,128)(2,1)} %bitcast.9), calls=%async_computation | async-start | bytes 3276800 | tf_op jit(solution)/shard_map/all_to_all | solution.py:256

commit v4 on v3

--- a/solution.py
+++ b/solution.py
@@ -41,8 +41,8 @@
         )
     ids_copy = pltpu.make_async_copy(ids_hbm, ids_ref, ids_sem)
     ids_copy.start()
-    for copy in x_copies:
-        copy.start()
+    for g, copy in enumerate(x_copies):
+        copy.start(priority=2 * g // steps)
     block = (PEERS - 1 - lax.axis_index("expert")) % QUAD
     line = iota((QUAD * LINES, LANES), 0)
     owner = line * 0
@@ -80,9 +80,10 @@
     )
     counts = jnp.concatenate([counts, counts], axis=1)
     upper = iota((16, 2 * LANES), 0) < 8
-    for copy in x_copies:
-        copy.wait()
     for g in range(steps):
+        if g % (steps // 2) == 0:
+            for copy in x_copies[g : g + steps // 2]:
+                copy.wait()
         one = x_ref[pl.ds(g * rows, rows // 2), :]
         two = x_ref[pl.ds(g * rows + rows // 2, rows // 2), :]
         thirds = []
@@ -109,9 +110,7 @@
         start = (steps - 1 - g) * 2 * OCT * LINES
         out_ref[pl.ds(start + OCT * LINES, OCT * LINES), :] = packed[:, :LANES]
         out_ref[pl.ds(start, OCT * LINES), :] = packed[:, LANES:]
-        if g % 2:
-            out_copies[g - 1].start()
-            out_copies[g].start()
+        out_copies[g].start()
     for copy in out_copies:
         copy.wait()
 

time: 63.3 us -> 63.2 us (level)
  no operation moved by 1% of the time
where the time goes in v4:
time: 63.2 us; the launch traced here: 62.9 us
  waiting for transfers between devices  39.2 us (62%)
  starting transfers between devices  18.1 us (29%)
  Pallas kernels  4.91 us (8%)
  between operations  0.69 us (1%)
    all_to_all x1, waiting for transfers between devices, per_device(): lax.all_to_all(packed.reshape(PEERS, LINES // 2, 2, LANES), 'expert', spl...  39.2 us
    all_to_all x1, starting transfers between devices, per_device(): lax.all_to_all(packed.reshape(PEERS, LINES // 2, 2, LANES), 'expert', spl...  18.1 us
    pallas_call x1, Pallas kernels, per_device(): pl.pallas_call(pack_kernel, out_shape=jax.ShapeDtypeStruct((PEERS * LINES...  2.93 us
    pallas_call x1, Pallas kernels, per_device(): pl.pallas_call(combine_kernel, out_shape=(jax.ShapeDtypeStruct((TOK, widt...  1.29 us
  transfers between devices with their start and end apart: 1, of which 1 were waited for; matrix products, arithmetic and copies ran while one was open for 0% of the time, Pallas kernels for 1%

profile of v4, /device:TPU:6, one launch (start us, length us, event | category | flops | bytes accessed | tf_op | source)
XLA Modules:
  0.0 62.9 jit_solution(11465683412124091996)
XLA Ops:
  0.6 2.9 %pack.1 = bf16[6400,128]{1,0:T(8,128)(2,1)} custom-call(bf16[768,1024]{1,0:T(8,128)(2,1)} %x_hbm.1, s32[8,64]{1,0:T(8,128)} %bitcast.6), custom_call_target="tpu_custom_call" | custom-call | tf_op jit(solution)/shard_map/pack/pallas_call | solution.py:239
  3.6 0.0 copy-start.1
  3.6 0.0 copy-start.2
  3.6 0.0 copy-start
  3.6 18.1 %all-to-all-start = ((bf16[128,25,2,128]{3,2,1,0:T(2,128)(2,1)}), bf16[128,25,2,128]{3,2,1,0:T(2,128)(2,1)S(1)}, u32[]{:S(2)}, u32[]{:S(2)}) async-start(bf16[128,25,2,128]{3,2,1,0:T(2,128)(2,1)} %bitcast.9), calls=%async_computation | async-start | bytes 3276800 | tf_op jit(solution)/shard_map/all_to_all | solution.py:255
  21.7 0.0 copy-done.1
  21.7 0.0 copy-done.2
  21.8 0.7 %weights.1 = (bf16[4,128,1024]{2,1,0:T(8,128)(2,1)S(1)}, bf16[384,256]{1,0:T(8,128)(2,1)S(1)}) custom-call(s32[8,64]{1,0:T(8,128)S(1)} %bitcast.7, f32[8,64]{1,0:T(8,128)S(1)} %bitcast.8), custom_call_target="tpu_custom_call" | custom-call | tf_op jit(solution)/shard_map/weights/pallas_call | solution.py:263
  22.4 39.2 %all-to-all-done = bf16[128,25,2,128]{3,2,1,0:T(2,128)(2,1)S(1)} async-done(((bf16[128,25,2,128]{3,2,1,0:T(2,128)(2,1)}), bf16[128,25,2,128]{3,2,1,0:T(2,128)(2,1)S(1)}, u32[]{:S(2)}, u32[]{:S(2)}) %all-to-all-start) | async-done | bytes 1638432 | tf_op jit(solution)/shard_map/all_to_all | solution.py:255
  61.6 0.0 copy-done
  61.6 1.3 %combine.1 = (bf16[64,1024]{1,0:T(8,128)(2,1)}, f32[1,64]{1,0:T(1,128)}) custom-call(bf16[4,128,1024]{2,1,0:T(8,128)(2,1)S(1)} %get-tuple-element.6.weights_ref, bf16[384,256]{1,0:T(8,128)(2,1)S(1)} %get-tuple-element.7.odd_ref, bf16[32,25,8,128]{3,2,1,0:T(8,128)(2,1)S(1)} %bitcast.5, bf16[64,1024]{1,0:T(8,128)(2,1)S(1)} %copy-done), custom_call_target="tpu_custom_call" | custom-call | tf_op jit(solution)/shard_map/combine/pallas_call | solution.py:274
Async XLA Ops:
  3.6 18.2 %copy-start.1 = (s32[64,8]{0,1:T(8,128)S(1)}, s32[64,8]{0,1:T(8,128)}, u32[]{:S(2)}) copy-start(s32[64,8]{0,1:T(8,128)} %param.5) | copy-start | bytes 6148
  3.6 18.2 %copy-start.2 = (f32[64,8]{0,1:T(8,128)S(1)}, f32[64,8]{0,1:T(8,128)}, u32[]{:S(2)}) copy-start(f32[64,8]{0,1:T(8,128)} %param.6) | copy-start | bytes 6148
  3.6 58.1 %copy-start = (bf16[64,1024]{1,0:T(8,128)(2,1)S(1)}, bf16[64,1024]{1,0:T(8,128)(2,1)}, u32[]{:S(2)}) copy-start(bf16[64,1024]{1,0:T(8,128)(2,1)} %residual_ref.1) | copy-start | bytes 393220
  3.6 58.0 %all-to-all-start = ((bf16[128,25,2,128]{3,2,1,0:T(2,128)(2,1)}), bf16[128,25,2,128]{3,2,1,0:T(2,128)(2,1)S(1)}, u32[]{:S(2)}, u32[]{:S(2)}) async-start(bf16[128,25,2,128]{3,2,1,0:T(2,128)(2,1)} %bitcast.9), calls=%async_computation | async-start | bytes 3276800 | tf_op jit(solution)/shard_map/all_to_all | solution.py:255

commit v5 on v4

--- a/solution.py
+++ b/solution.py
@@ -31,18 +31,19 @@
 def pack_kernel(x_hbm, ids_hbm, out_hbm, x_ref, ids_ref, out_ref, x_sems, ids_sem, out_sems):
     rows = 2 * OCT * HELD
     steps = PEERS // (2 * OCT)
-    x_copies, out_copies = [], []
+    x_copies, out_copies = {}, []
+    for i, (g, end) in enumerate(((0, 3), (3, steps))):
+        here = pl.ds(g * rows, (end - g) * rows)
+        x_copies[g] = pltpu.make_async_copy(x_hbm.at[here], x_ref.at[here], x_sems.at[i])
     for g in range(steps):
-        here = pl.ds(g * rows, rows)
         there = pl.ds((steps - 1 - g) * 2 * OCT * LINES, 2 * OCT * LINES)
-        x_copies.append(pltpu.make_async_copy(x_hbm.at[here], x_ref.at[here], x_sems.at[g]))
         out_copies.append(
             pltpu.make_async_copy(out_ref.at[there], out_hbm.at[there], out_sems.at[g])
         )
     ids_copy = pltpu.make_async_copy(ids_hbm, ids_ref, ids_sem)
     ids_copy.start()
-    for g, copy in enumerate(x_copies):
-        copy.start(priority=2 * g // steps)
+    for i, copy in enumerate(x_copies.values()):
+        copy.start(priority=i)
     block = (PEERS - 1 - lax.axis_index("expert")) % QUAD
     line = iota((QUAD * LINES, LANES), 0)
     owner = line * 0
@@ -81,9 +82,8 @@
     counts = jnp.concatenate([counts, counts], axis=1)
     upper = iota((16, 2 * LANES), 0) < 8
     for g in range(steps):
-        if g % (steps // 2) == 0:
-            for copy in x_copies[g : g + steps // 2]:
-                copy.wait()
+        if g in x_copies:
+            x_copies[g].wait()
         one = x_ref[pl.ds(g * rows, rows // 2), :]
         two = x_ref[pl.ds(g * rows + rows // 2, rows // 2), :]
         thirds = []
@@ -245,7 +245,7 @@
             pltpu.VMEM(expert_out.shape, jnp.bfloat16),
             pltpu.VMEM(ids.shape, jnp.int32),
             pltpu.VMEM((PEERS * LINES, LANES), jnp.bfloat16),
-            pltpu.SemaphoreType.DMA((steps,)),
+            pltpu.SemaphoreType.DMA((2,)),
             pltpu.SemaphoreType.DMA,
             pltpu.SemaphoreType.DMA((steps,)),
         ],

time: 63.2 us -> 63 us (level)
  no operation moved by 1% of the time
where the time goes in v5:
time: 63 us; the launch traced here: 62.8 us
  waiting for transfers between devices  39.2 us (62%)
  starting transfers between devices  18.1 us (29%)
  Pallas kernels  4.73 us (8%)
  between operations  0.69 us (1%)
    all_to_all x1, waiting for transfers between devices, per_device(): lax.all_to_all(packed.reshape(PEERS, LINES // 2, 2, LANES), 'expert', spl...  39.2 us
    all_to_all x1, starting transfers between devices, per_device(): lax.all_to_all(packed.reshape(PEERS, LINES // 2, 2, LANES), 'expert', spl...  18.1 us
    pallas_call x1, Pallas kernels, per_device(): pl.pallas_call(pack_kernel, out_shape=jax.ShapeDtypeStruct((PEERS * LINES...  2.75 us
    pallas_call x1, Pallas kernels, per_device(): pl.pallas_call(combine_kernel, out_shape=(jax.ShapeDtypeStruct((TOK, widt...  1.29 us
  transfers between devices with their start and end apart: 1, of which 1 were waited for; matrix products, arithmetic and copies ran while one was open for 0% of the time, Pallas kernels for 1%

profile of v5, /device:TPU:6, one launch (start us, length us, event | category | flops | bytes accessed | tf_op | source)
XLA Modules:
  0.0 62.8 jit_solution(10927689410197581019)
XLA Ops:
  0.6 2.8 %pack.1 = bf16[6400,128]{1,0:T(8,128)(2,1)} custom-call(bf16[768,1024]{1,0:T(8,128)(2,1)} %x_hbm.1, s32[8,64]{1,0:T(8,128)} %bitcast.6), custom_call_target="tpu_custom_call" | custom-call | tf_op jit(solution)/shard_map/pack/pallas_call | solution.py:239
  3.4 0.0 copy-start.1
  3.4 0.0 copy-start.2
  3.4 0.0 copy-start
  3.4 18.1 %all-to-all-start = ((bf16[128,25,2,128]{3,2,1,0:T(2,128)(2,1)}), bf16[128,25,2,128]{3,2,1,0:T(2,128)(2,1)S(1)}, u32[]{:S(2)}, u32[]{:S(2)}) async-start(bf16[128,25,2,128]{3,2,1,0:T(2,128)(2,1)} %bitcast.9), calls=%async_computation | async-start | bytes 3276800 | tf_op jit(solution)/shard_map/all_to_all | solution.py:255
  21.5 0.0 copy-done.1
  21.6 0.0 copy-done.2
  21.6 0.7 %weights.1 = (bf16[4,128,1024]{2,1,0:T(8,128)(2,1)S(1)}, bf16[384,256]{1,0:T(8,128)(2,1)S(1)}) custom-call(s32[8,64]{1,0:T(8,128)S(1)} %bitcast.7, f32[8,64]{1,0:T(8,128)S(1)} %bitcast.8), custom_call_target="tpu_custom_call" | custom-call | tf_op jit(solution)/shard_map/weights/pallas_call | solution.py:263
  22.3 39.2 %all-to-all-done = bf16[128,25,2,128]{3,2,1,0:T(2,128)(2,1)S(1)} async-done(((bf16[128,25,2,128]{3,2,1,0:T(2,128)(2,1)}), bf16[128,25,2,128]{3,2,1,0:T(2,128)(2,1)S(1)}, u32[]{:S(2)}, u32[]{:S(2)}) %all-to-all-start) | async-done | bytes 1638432 | tf_op jit(solution)/shard_map/all_to_all | solution.py:255
  61.5 0.0 copy-done
  61.5 1.3 %combine.1 = (bf16[64,1024]{1,0:T(8,128)(2,1)}, f32[1,64]{1,0:T(1,128)}) custom-call(bf16[4,128,1024]{2,1,0:T(8,128)(2,1)S(1)} %get-tuple-element.6.weights_ref, bf16[384,256]{1,0:T(8,128)(2,1)S(1)} %get-tuple-element.7.odd_ref, bf16[32,25,8,128]{3,2,1,0:T(8,128)(2,1)S(1)} %bitcast.5, bf16[64,1024]{1,0:T(8,128)(2,1)S(1)} %copy-done), custom_call_target="tpu_custom_call" | custom-call | tf_op jit(solution)/shard_map/combine/pallas_call | solution.py:274
Async XLA Ops:
  3.4 18.2 %copy-start.1 = (s32[64,8]{0,1:T(8,128)S(1)}, s32[64,8]{0,1:T(8,128)}, u32[]{:S(2)}) copy-start(s32[64,8]{0,1:T(8,128)} %param.5) | copy-start | bytes 6148
  3.4 18.2 %copy-start.2 = (f32[64,8]{0,1:T(8,128)S(1)}, f32[64,8]{0,1:T(8,128)}, u32[]{:S(2)}) copy-start(f32[64,8]{0,1:T(8,128)} %param.6) | copy-start | bytes 6148
  3.4 58.0 %copy-start = (bf16[64,1024]{1,0:T(8,128)(2,1)S(1)}, bf16[64,1024]{1,0:T(8,128)(2,1)}, u32[]{:S(2)}) copy-start(bf16[64,1024]{1,0:T(8,128)(2,1)} %residual_ref.1) | copy-start | bytes 393220
  3.4 58.0 %all-to-all-start = ((bf16[128,25,2,128]{3,2,1,0:T(2,128)(2,1)}), bf16[128,25,2,128]{3,2,1,0:T(2,128)(2,1)S(1)}, u32[]{:S(2)}, u32[]{:S(2)}) async-start(bf16[128,25,2,128]{3,2,1,0:T(2,128)(2,1)} %bitcast.9), calls=%async_computation | async-start | bytes 3276800 | tf_op jit(solution)/shard_map/all_to_all | solution.py:255

commit v6 on v5

--- a/solution.py
+++ b/solution.py
@@ -110,7 +110,7 @@
         start = (steps - 1 - g) * 2 * OCT * LINES
         out_ref[pl.ds(start + OCT * LINES, OCT * LINES), :] = packed[:, :LANES]
         out_ref[pl.ds(start, OCT * LINES), :] = packed[:, LANES:]
-        out_copies[g].start()
+        out_copies[g].start(priority=g % 2)
     for copy in out_copies:
         copy.wait()
 

time: 63 us -> 63 us (level)
  no operation moved by 1% of the time
where the time goes in v6:
time: 63 us; the launch traced here: 62.8 us
  waiting for transfers between devices  39.2 us (62%)
  starting transfers between devices  18.1 us (29%)
  Pallas kernels  4.73 us (8%)
  between operations  0.69 us (1%)
    all_to_all x1, waiting for transfers between devices, per_device(): lax.all_to_all(packed.reshape(PEERS, LINES // 2, 2, LANES), 'expert', spl...  39.2 us
    all_to_all x1, starting transfers between devices, per_device(): lax.all_to_all(packed.reshape(PEERS, LINES // 2, 2, LANES), 'expert', spl...  18.1 us
    pallas_call x1, Pallas kernels, per_device(): pl.pallas_call(pack_kernel, out_shape=jax.ShapeDtypeStruct((PEERS * LINES...  2.75 us
    pallas_call x1, Pallas kernels, per_device(): pl.pallas_call(combine_kernel, out_shape=(jax.ShapeDtypeStruct((TOK, widt...  1.29 us
  transfers between devices with their start and end apart: 1, of which 1 were waited for; matrix products, arithmetic and copies ran while one was open for 0% of the time, Pallas kernels for 1%

profile of v6, /device:TPU:6, one launch (start us, length us, event | category | flops | bytes accessed | tf_op | source)
XLA Modules:
  0.0 62.8 jit_solution(2377480022061342596)
XLA Ops:
  0.6 2.8 %pack.1 = bf16[6400,128]{1,0:T(8,128)(2,1)} custom-call(bf16[768,1024]{1,0:T(8,128)(2,1)} %x_hbm.1, s32[8,64]{1,0:T(8,128)} %bitcast.6), custom_call_target="tpu_custom_call" | custom-call | tf_op jit(solution)/shard_map/pack/pallas_call | solution.py:239
  3.4 0.0 copy-start.1
  3.4 0.0 copy-start.2
  3.4 0.0 copy-start
  3.4 18.1 %all-to-all-start = ((bf16[128,25,2,128]{3,2,1,0:T(2,128)(2,1)}), bf16[128,25,2,128]{3,2,1,0:T(2,128)(2,1)S(1)}, u32[]{:S(2)}, u32[]{:S(2)}) async-start(bf16[128,25,2,128]{3,2,1,0:T(2,128)(2,1)} %bitcast.9), calls=%async_computation | async-start | bytes 3276800 | tf_op jit(solution)/shard_map/all_to_all | solution.py:255
  21.5 0.0 copy-done.1
  21.6 0.0 copy-done.2
  21.6 0.7 %weights.1 = (bf16[4,128,1024]{2,1,0:T(8,128)(2,1)S(1)}, bf16[384,256]{1,0:T(8,128)(2,1)S(1)}) custom-call(s32[8,64]{1,0:T(8,128)S(1)} %bitcast.7, f32[8,64]{1,0:T(8,128)S(1)} %bitcast.8), custom_call_target="tpu_custom_call" | custom-call | tf_op jit(solution)/shard_map/weights/pallas_call | solution.py:263
  22.3 39.2 %all-to-all-done = bf16[128,25,2,128]{3,2,1,0:T(2,128)(2,1)S(1)} async-done(((bf16[128,25,2,128]{3,2,1,0:T(2,128)(2,1)}), bf16[128,25,2,128]{3,2,1,0:T(2,128)(2,1)S(1)}, u32[]{:S(2)}, u32[]{:S(2)}) %all-to-all-start) | async-done | bytes 1638432 | tf_op jit(solution)/shard_map/all_to_all | solution.py:255
  61.5 0.0 copy-done
  61.5 1.3 %combine.1 = (bf16[64,1024]{1,0:T(8,128)(2,1)}, f32[1,64]{1,0:T(1,128)}) custom-call(bf16[4,128,1024]{2,1,0:T(8,128)(2,1)S(1)} %get-tuple-element.6.weights_ref, bf16[384,256]{1,0:T(8,128)(2,1)S(1)} %get-tuple-element.7.odd_ref, bf16[32,25,8,128]{3,2,1,0:T(8,128)(2,1)S(1)} %bitcast.5, bf16[64,1024]{1,0:T(8,128)(2,1)S(1)} %copy-done), custom_call_target="tpu_custom_call" | custom-call | tf_op jit(solution)/shard_map/combine/pallas_call | solution.py:274
Async XLA Ops:
  3.4 18.2 %copy-start.1 = (s32[64,8]{0,1:T(8,128)S(1)}, s32[64,8]{0,1:T(8,128)}, u32[]{:S(2)}) copy-start(s32[64,8]{0,1:T(8,128)} %param.5) | copy-start | bytes 6148
  3.4 18.2 %copy-start.2 = (f32[64,8]{0,1:T(8,128)S(1)}, f32[64,8]{0,1:T(8,128)}, u32[]{:S(2)}) copy-start(f32[64,8]{0,1:T(8,128)} %param.6) | copy-start | bytes 6148
  3.4 58.0 %copy-start = (bf16[64,1024]{1,0:T(8,128)(2,1)S(1)}, bf16[64,1024]{1,0:T(8,128)(2,1)}, u32[]{:S(2)}) copy-start(bf16[64,1024]{1,0:T(8,128)(2,1)} %residual_ref.1) | copy-start | bytes 393220
  3.4 58.0 %all-to-all-start = ((bf16[128,25,2,128]{3,2,1,0:T(2,128)(2,1)}), bf16[128,25,2,128]{3,2,1,0:T(2,128)(2,1)S(1)}, u32[]{:S(2)}, u32[]{:S(2)}) async-start(bf16[128,25,2,128]{3,2,1,0:T(2,128)(2,1)} %bitcast.9), calls=%async_computation | async-start | bytes 3276800 | tf_op jit(solution)/shard_map/all_to_all | solution.py:255
